TPU v7x, 256 devices: a whole 4x4x8 slice. The times are simulated.
256 devices in a mesh: win: 16 (over z, y_lo), seq: 16 (over x, y_hi, core).
Axes of the slice: x: 4, y: 4 (y_hi: 2, y_lo: 2; y = y_hi * 2 + y_lo), z: 8, core: 2. Of those that a mesh axis runs over, the one named last changes fastest.
Arguments:
- queries: bfloat16 [2, 16, 2048, 2048], P(None, 'win', 'seq'), may hold values from -4.5 to 4.5
- key_states: bfloat16 [2, 16, 2048, 2048], P(None, 'win', 'seq'), may hold values from -4.5 to 4.5
- value_states: bfloat16 [2, 16, 2048, 2048], P(None, 'win', 'seq'), may hold values from -5 to 5
- out_grad: bfloat16 [2, 16, 2048, 2048], P(None, 'win', 'seq'), may hold values from -60 to 60
Outputs:
- query_grad: bfloat16 [2, 16, 2048, 2048], P(None, 'win', 'seq')
- key_grad: bfloat16 [2, 16, 2048, 2048], P(None, 'win', 'seq')
- value_grad: bfloat16 [2, 16, 2048, 2048], P(None, 'win', 'seq')
All inputs are finite; a program needn't handle non-finite values.
Results may differ from a plain program's by a relative error of at most 0.0095.
Values may be sent and summed in bfloat16 or wider, within the bound.
A program may use at most 128 MiB of HBM per device.

v0:
```python
import jax
import jax.numpy as jnp
from jax import lax
from jax.sharding import Mesh
from jax.sharding import PartitionSpec as P

HEADS = 16
HDIM = 128
ROWS = 32
COLS = 64
SEQ = ("seq_0", "seq_1", "seq_2")


def passed_along(block, axis, distance):
    devices = range(lax.axis_size(axis))
    route = [((i - distance) % len(devices), i) for i in devices]
    return lax.ppermute(block, axis, route)


def split_up(value, dim, peers):
    before, after = (value.shape[:dim], value.shape[dim + 1 :])
    return jnp.moveaxis(value.reshape(*before, peers, -1, *after), dim, 0)


def joined_along(pieces, dim):
    pieces = jnp.moveaxis(pieces, 0, dim)
    dims = pieces.shape
    return pieces.reshape(*dims[:dim], dims[dim] * dims[dim + 1], *dims[dim + 2 :])


def exchange_in_order(pieces, axes, turns):
    inside = pieces.shape[1:]
    result = pieces.reshape(*(lax.axis_size(a) for a in axes), *inside)
    for k in turns:
        result = lax.all_to_all(result, axes[k], k, k, tiled=True)
    return result.reshape(-1, *inside)


def two_step_exchange(value, groups, turns, split_dim, concat_dim):
    peers = lax.axis_size(groups[0]) * lax.axis_size(groups[1])
    pieces = split_up(value, split_dim, peers)
    return joined_along(exchange_in_order(pieces, groups, turns), concat_dim)


def items_in_groups(value, axis, split_dim, concat_dim, work, item_dim, out_dim):
    items = jax.tree.leaves(value)[0].shape[item_dim]
    count = 2 if items % 2 == 0 else 1
    done = []
    for k in range(count):
        group = jax.tree.map(
            lambda a: lax.slice_in_dim(
                a, k * (items // count), (k + 1) * (items // count), axis=item_dim
            ),
            value,
        )
        done.append(
            work(
                lax.all_to_all(
                    group, axis, split_axis=split_dim, concat_axis=concat_dim, tiled=True
                )
            )
        )
    return jax.tree.map(lambda *parts: jnp.concatenate(parts, axis=out_dim), *done)


def ahead_columns(values, col_axis):
    middle = values.shape[col_axis] // 2
    arrived = passed_along(lax.slice_in_dim(values, 0, middle, axis=col_axis), "win", -1)
    return jnp.concatenate(
        [lax.slice_in_dim(values, middle, 2 * middle, axis=col_axis), arrived], axis=col_axis
    )


def behind_columns(values, col_axis):
    middle = values.shape[col_axis] // 2
    arrived = passed_along(lax.slice_in_dim(values, middle, 2 * middle, axis=col_axis), "win", 1)
    return jnp.concatenate(
        [arrived, lax.slice_in_dim(values, 0, middle, axis=col_axis)], axis=col_axis
    )


def back_to_tokens(gradients):
    return two_step_exchange(gradients, (("seq_0", "seq_1"), "seq_2"), (1, 0), 2, 3)


def window_grads(query_heads, key_heads, value_heads, grad_heads):
    samples_here, tokens, own_heads, head_size = query_heads.shape
    block_rows = min(512, tokens)
    factor = head_size ** (-0.5)

    def one_block(totals, offset):
        key_total, value_total = totals
        query_block = lax.dynamic_slice_in_dim(query_heads, offset, block_rows, 1)
        grad_block = lax.dynamic_slice_in_dim(grad_heads, offset, block_rows, 1)
        scores = (
            jnp.einsum(
                "bqhd,bkhd->bhqk", query_block, key_heads, preferred_element_type=jnp.float32
            )
            * factor
        )
        scores = scores - jnp.max(scores, axis=3, keepdims=True)
        weights = jnp.exp(scores)
        weights = weights / jnp.sum(weights, axis=3, keepdims=True)
        weights_low = weights.astype(jnp.bfloat16)
        value_total = value_total + jnp.einsum(
            "bhqk,bqhd->bkhd", weights_low, grad_block, preferred_element_type=jnp.float32
        )
        grad_probs = jnp.einsum(
            "bqhd,bkhd->bhqk", grad_block, value_heads, preferred_element_type=jnp.float32
        )
        row_dot = jnp.sum(weights * grad_probs, axis=3, keepdims=True)
        grad_scores = (weights * (grad_probs - row_dot) * factor).astype(jnp.bfloat16)
        query_block_grad = jnp.einsum(
            "bhqk,bkhd->bqhd", grad_scores, key_heads, preferred_element_type=jnp.float32
        ).astype(jnp.bfloat16)
        key_total = key_total + jnp.einsum(
            "bhqk,bqhd->bkhd", grad_scores, query_block, preferred_element_type=jnp.float32
        )
        return ((key_total, value_total), query_block_grad)

    starts = jnp.arange(tokens // block_rows, dtype=jnp.int32) * block_rows
    zero_acc = jnp.zeros(query_heads.shape, jnp.float32)
    (key_total, value_total), query_blocks = lax.scan(one_block, (zero_acc, zero_acc), starts)
    query_grad = jnp.moveaxis(query_blocks, 0, 1).reshape(
        samples_here, tokens, own_heads, head_size
    )
    return jnp.stack([query_grad, key_total.astype(jnp.bfloat16), value_total.astype(jnp.bfloat16)])


def on_device(queries, key_states, value_states, out_grad):
    samples = queries.shape[0]
    local_tokens = queries.shape[2]
    model_width = queries.shape[3]

    def head_view(values):
        return values.reshape(samples, local_tokens, HEADS, HDIM)

    sent_grad = head_view(out_grad)

    def per_items(received):
        query_heads, key_heads, value_heads, grad_heads = received
        item_count, tokens, own_heads, head_size = query_heads.shape
        head_grid = grad_heads.reshape(item_count, ROWS, COLS, own_heads, head_size)
        head_grid = jnp.roll(ahead_columns(head_grid, 2), -(ROWS // 2), axis=1)
        grad_heads = head_grid.reshape(item_count, tokens, own_heads, head_size)
        gradients = window_grads(query_heads, key_heads, value_heads, grad_heads)
        back_grid = gradients.reshape(3, item_count, ROWS, COLS, own_heads, head_size)
        back_grid = behind_columns(jnp.roll(back_grid, ROWS // 2, axis=2), 3)
        gradients = back_grid.reshape(3, item_count, tokens, own_heads, head_size)
        return gradients

    result = items_in_groups(
        (head_view(queries), head_view(key_states), head_view(value_states), sent_grad),
        SEQ,
        2,
        1,
        per_items,
        0,
        1,
    )
    result = back_to_tokens(result)
    pieces = result.reshape(3, samples, 1, local_tokens, model_width)
    return (pieces[0], pieces[1], pieces[2])


def solution(mesh):
    torus = Mesh(
        mesh.devices.reshape(mesh.shape["win"], 4, 2, 2), ("win", "seq_0", "seq_1", "seq_2")
    )
    in_specs = (
        P(None, "win", SEQ, None),
        P(None, "win", SEQ, None),
        P(None, "win", SEQ, None),
        P(None, "win", SEQ, None),
    )
    out_specs = (P(None, "win", SEQ, None), P(None, "win", SEQ, None), P(None, "win", SEQ, None))
    return jax.shard_map(
        on_device, mesh=torus, in_specs=in_specs, out_specs=out_specs, check_vma=False
    )
```

profile of v0, /device:TPU:104, one launch (start us, length us, event | category | flops | bytes accessed | tf_op | source)
XLA Modules:
  0.0 389.2 jit_solution(14366073978462145350)
XLA Ops:
  3.3 6.1 %all-to-all-start.2 = ((bf16[1,128,16,128]{3,1,0,2:T(8,128)(2,1)}), bf16[1,128,16,128]{3,1,0,2:T(8,128)(2,1)S(1)}, u32[]{:S(2)}, u32[]{:S(2)}) async-start(bf16[1,128,16,128]{3,1,0,2:T(8,128)(2,1)} %copy.107), calls=%async_computation.2 | async-start | bytes 1048576 | tf_op jit(solution)/shard_map/all_to_all | solution.py:58
  11.4 10.4 %all-to-all-done.2 = bf16[1,128,16,128]{3,1,0,2:T(8,128)(2,1)S(1)} async-done(((bf16[1,128,16,128]{3,1,0,2:T(8,128)(2,1)}), bf16[1,128,16,128]{3,1,0,2:T(8,128)(2,1)S(1)}, u32[]{:S(2)}, u32[]{:S(2)}) %all-to-all-start.2) | async-done | bytes 524320 | tf_op jit(solution)/shard_map/all_to_all | solution.py:58
  21.8 3.6 all-to-all-start.3
  25.4 2.1 fusion.64
  28.5 9.2 %all-to-all-done.3 = bf16[1,128,16,128]{1,3,0,2:T(8,128)(2,1)S(1)} async-done(((bf16[1,128,16,128]{1,3,0,2:T(8,128)(2,1)}), bf16[1,128,16,128]{1,3,0,2:T(8,128)(2,1)S(1)}, u32[]{:S(2)}, u32[]{:S(2)}) %all-to-all-start.3) | async-done | bytes 524320 | tf_op jit(solution)/shard_map/all_to_all | solution.py:58
  37.7 3.6 all-to-all-start
  41.3 2.1 fusion.63
  44.4 9.2 %all-to-all-done = bf16[1,128,16,128]{1,3,0,2:T(8,128)(2,1)S(1)} async-done(((bf16[1,128,16,128]{1,3,0,2:T(8,128)(2,1)}), bf16[1,128,16,128]{1,3,0,2:T(8,128)(2,1)S(1)}, u32[]{:S(2)}, u32[]{:S(2)}) %all-to-all-start) | async-done | bytes 524320 | tf_op jit(solution)/shard_map/all_to_all | solution.py:58
  53.7 3.6 all-to-all-start.1
  58.5 11.0 %all-to-all-done.1 = bf16[1,128,16,128]{1,3,0,2:T(8,128)(2,1)S(1)} async-done(((bf16[1,128,16,128]{1,3,0,2:T(8,128)(2,1)}), bf16[1,128,16,128]{1,3,0,2:T(8,128)(2,1)S(1)}, u32[]{:S(2)}, u32[]{:S(2)}) %all-to-all-start.1) | async-done | bytes 524320 | tf_op jit(solution)/shard_map/all_to_all | solution.py:58
  69.6 3.6 all-to-all-start.6
  73.1 2.0 copy.142
  75.2 10.3 %all-to-all-done.6 = bf16[1,128,16,128]{3,1,0,2:T(8,128)(2,1)S(1)} async-done(((bf16[1,128,16,128]{3,1,0,2:T(8,128)(2,1)}), bf16[1,128,16,128]{3,1,0,2:T(8,128)(2,1)S(1)}, u32[]{:S(2)}, u32[]{:S(2)}) %all-to-all-start.6) | async-done | bytes 524320 | tf_op jit(solution)/shard_map/all_to_all | solution.py:58
  85.5 3.6 all-to-all-start.4
  89.0 2.0 copy.143
  91.1 10.3 %all-to-all-done.4 = bf16[1,128,16,128]{1,3,0,2:T(8,128)(2,1)S(1)} async-done(((bf16[1,128,16,128]{1,3,0,2:T(8,128)(2,1)}), bf16[1,128,16,128]{1,3,0,2:T(8,128)(2,1)S(1)}, u32[]{:S(2)}, u32[]{:S(2)}) %all-to-all-start.4) | async-done | bytes 524320 | tf_op jit(solution)/shard_map/all_to_all | solution.py:58
  101.4 4.2 %all-to-all-start.5 = ((bf16[1,128,16,128]{1,3,0,2:T(8,128)(2,1)}), bf16[1,128,16,128]{1,3,0,2:T(8,128)(2,1)}, u32[]{:S(2)}, u32[]{:S(2)}) async-start(bf16[1,128,16,128]{1,3,0,2:T(8,128)(2,1)} %bitcast.248), calls=%async_computation.5 | async-start | bytes 1048576 | tf_op jit(solution)/shard_map/all_to_all | solution.py:58
  105.6 2.0 copy.145
  107.7 10.3 %all-to-all-done.5 = bf16[1,128,16,128]{1,3,0,2:T(8,128)(2,1)} async-done(((bf16[1,128,16,128]{1,3,0,2:T(8,128)(2,1)}), bf16[1,128,16,128]{1,3,0,2:T(8,128)(2,1)}, u32[]{:S(2)}, u32[]{:S(2)}) %all-to-all-start.5) | async-done | bytes 524320 | tf_op jit(solution)/shard_map/all_to_all | solution.py:58
  118.0 4.2 %all-to-all-start.7 = ((bf16[1,128,16,128]{1,3,0,2:T(8,128)(2,1)}), bf16[1,128,16,128]{1,3,0,2:T(8,128)(2,1)}, u32[]{:S(2)}, u32[]{:S(2)}) async-start(bf16[1,128,16,128]{1,3,0,2:T(8,128)(2,1)} %bitcast.246), calls=%async_computation.7 | async-start | bytes 1048576 | tf_op jit(solution)/shard_map/all_to_all | solution.py:58
  129.8 2.1 copy.115
  134.6 2.1 copy.123
  141.8 72.6 %while.30 = (s32[]{:T(128)}, f32[1,2048,1,128]{1,3,2,0:T(8,128)S(1)}, f32[1,2048,1,128]{1,3,2,0:T(8,128)}, bf16[4,1,512,1,128]{4,2,3,1,0:T(8,128)(2,1)}, s32[4]{...) while((s32[]{:T(128)}, ...), condition=%wide.region_4.5_spmd.clone, body=%wide.region_0.4_spmd.clone.sunk | while | flops 1365309952 | bytes 77749016 | solution.py:123
  148.6 4.5 %fusion.99 = f32[1,2048,1,128]{1,3,2,0:T(8,128)} fusion(f32[1,2048,1,128]{1,3,2,0:T(8,128)} %get-tuple-element.409, pred[]{:T(512)S(6)} %compare.6, bf16[1,2048,1,128]{3,1,2,0:T(8,128)(2,1)} %get-tuple-element.426, s32[]{:T(128)S(6)} %select_n.12, f32[512,2048]{1,0:T(8,128)} %copy-done, f32[512]{0:T(512)S(1)} %fusion.97, f32[512]{0:T(512)S(1)} %get-tuple-element.343), kind=kOutput, calls=%fused_computation.9.clone.1 | convolution fusion | flops 273154048 | bytes 6426629 | tf_op jit(solution)/shard_map/while/body/eval_jaxpr/bhqk,bqhd->bkhd/dot_general | solution.py:105
  153.2 2.2 multiply_reduce_fusion.9
  166.6 4.8 %fusion.99 = f32[1,2048,1,128]{1,3,2,0:T(8,128)} fusion(f32[1,2048,1,128]{1,3,2,0:T(8,128)} %get-tuple-element.409, pred[]{:T(512)S(6)} %compare.6, bf16[1,2048,1,128]{3,1,2,0:T(8,128)(2,1)} %get-tuple-element.426, s32[]{:T(128)S(6)} %select_n.12, f32[512,2048]{1,0:T(8,128)} %copy-done, f32[512]{0:T(512)S(1)} %fusion.97, f32[512]{0:T(512)S(1)} %get-tuple-element.343), kind=kOutput, calls=%fused_computation.9.clone.1 | convolution fusion | flops 273154048 | bytes 6426629 | tf_op jit(solution)/shard_map/while/body/eval_jaxpr/bhqk,bqhd->bkhd/dot_general | solution.py:105
  171.4 2.2 multiply_reduce_fusion.9
  184.8 4.8 %fusion.99 = f32[1,2048,1,128]{1,3,2,0:T(8,128)} fusion(f32[1,2048,1,128]{1,3,2,0:T(8,128)} %get-tuple-element.409, pred[]{:T(512)S(6)} %compare.6, bf16[1,2048,1,128]{3,1,2,0:T(8,128)(2,1)} %get-tuple-element.426, s32[]{:T(128)S(6)} %select_n.12, f32[512,2048]{1,0:T(8,128)} %copy-done, f32[512]{0:T(512)S(1)} %fusion.97, f32[512]{0:T(512)S(1)} %get-tuple-element.343), kind=kOutput, calls=%fused_computation.9.clone.1 | convolution fusion | flops 273154048 | bytes 6426629 | tf_op jit(solution)/shard_map/while/body/eval_jaxpr/bhqk,bqhd->bkhd/dot_general | solution.py:105
  189.6 2.2 multiply_reduce_fusion.9
  203.0 4.8 %fusion.99 = f32[1,2048,1,128]{1,3,2,0:T(8,128)} fusion(f32[1,2048,1,128]{1,3,2,0:T(8,128)} %get-tuple-element.409, pred[]{:T(512)S(6)} %compare.6, bf16[1,2048,1,128]{3,1,2,0:T(8,128)(2,1)} %get-tuple-element.426, s32[]{:T(128)S(6)} %select_n.12, f32[512,2048]{1,0:T(8,128)} %copy-done, f32[512]{0:T(512)S(1)} %fusion.97, f32[512]{0:T(512)S(1)} %get-tuple-element.343), kind=kOutput, calls=%fused_computation.9.clone.1 | convolution fusion | flops 273154048 | bytes 6426629 | tf_op jit(solution)/shard_map/while/body/eval_jaxpr/bhqk,bqhd->bkhd/dot_general | solution.py:105
  207.9 2.2 multiply_reduce_fusion.9
  218.5 4.0 %collective-permute-start.1 = (bf16[3,1,32,32,1,128]{5,3,2,4,1,0:T(8,128)(2,1)}, bf16[3,1,32,32,1,128]{5,3,2,4,1,0:T(8,128)(2,1)}, u32[]{:S(2)}, u32[]{:S(2)}) collective-permute-start(bf16[3,1,32,32,1,128]{5,3,2,4,1,0:T(8,128)(2,1)} %fusion.53), channel_id=1, source_target_pairs={{240,0},{0,16},{16,32},{32,48},{48,64},{64,80},{80,96},{96,112},{1... | collective-permute-start | bytes 2359304 | tf_op jit(solution)/shard_map/ppermute | solution.py:17
  226.1 72.7 %while.31 = (s32[]{:T(128)}, f32[1,2048,1,128]{1,3,2,0:T(8,128)S(1)}, f32[1,2048,1,128]{1,3,2,0:T(8,128)}, bf16[4,1,512,1,128]{4,2,3,1,0:T(8,128)(2,1)}, s32[4]{...) while((s32[]{:T(128)}, ...), condition=%wide.region_9.10_spmd.clone, body=%wide.region_5.9_spmd.clone.sunk | while | flops 1365309952 | bytes 77749016 | solution.py:123
  230.0 2.0 copy-done.2
  232.9 4.5 %fusion.109 = f32[1,2048,1,128]{1,3,2,0:T(8,128)} fusion(f32[1,2048,1,128]{1,3,2,0:T(8,128)} %get-tuple-element.373, pred[]{:T(512)S(6)} %compare.7, bf16[1,2048,1,128]{3,1,2,0:T(8,128)(2,1)} %get-tuple-element.390, s32[]{:T(128)S(6)} %select_n.13, f32[512,2048]{1,0:T(8,128)} %copy-done.2, f32[512]{0:T(512)S(1)} %fusion.107, ...), kind=kOutput, calls=%fused_computation.40.clone.1 | convolution fusion | flops 273154048 | bytes 6426629 | tf_op jit(solution)/shard_map/while/body/eval_jaxpr/bhqk,bqhd->bkhd/dot_general | solution.py:105
  237.4 2.2 multiply_reduce_fusion.11
  248.0 2.0 copy-done.2
  250.8 4.8 %fusion.109 = f32[1,2048,1,128]{1,3,2,0:T(8,128)} fusion(f32[1,2048,1,128]{1,3,2,0:T(8,128)} %get-tuple-element.373, pred[]{:T(512)S(6)} %compare.7, bf16[1,2048,1,128]{3,1,2,0:T(8,128)(2,1)} %get-tuple-element.390, s32[]{:T(128)S(6)} %select_n.13, f32[512,2048]{1,0:T(8,128)} %copy-done.2, f32[512]{0:T(512)S(1)} %fusion.107, ...), kind=kOutput, calls=%fused_computation.40.clone.1 | convolution fusion | flops 273154048 | bytes 6426629 | tf_op jit(solution)/shard_map/while/body/eval_jaxpr/bhqk,bqhd->bkhd/dot_general | solution.py:105
  255.7 2.2 multiply_reduce_fusion.11
  266.2 2.0 copy-done.2
  269.0 4.8 %fusion.109 = f32[1,2048,1,128]{1,3,2,0:T(8,128)} fusion(f32[1,2048,1,128]{1,3,2,0:T(8,128)} %get-tuple-element.373, pred[]{:T(512)S(6)} %compare.7, bf16[1,2048,1,128]{3,1,2,0:T(8,128)(2,1)} %get-tuple-element.390, s32[]{:T(128)S(6)} %select_n.13, f32[512,2048]{1,0:T(8,128)} %copy-done.2, f32[512]{0:T(512)S(1)} %fusion.107, ...), kind=kOutput, calls=%fused_computation.40.clone.1 | convolution fusion | flops 273154048 | bytes 6426629 | tf_op jit(solution)/shard_map/while/body/eval_jaxpr/bhqk,bqhd->bkhd/dot_general | solution.py:105
  273.9 2.2 multiply_reduce_fusion.11
  284.4 2.0 copy-done.2
  287.3 4.8 %fusion.109 = f32[1,2048,1,128]{1,3,2,0:T(8,128)} fusion(f32[1,2048,1,128]{1,3,2,0:T(8,128)} %get-tuple-element.373, pred[]{:T(512)S(6)} %compare.7, bf16[1,2048,1,128]{3,1,2,0:T(8,128)(2,1)} %get-tuple-element.390, s32[]{:T(128)S(6)} %select_n.13, f32[512,2048]{1,0:T(8,128)} %copy-done.2, f32[512]{0:T(512)S(1)} %fusion.107, ...), kind=kOutput, calls=%fused_computation.40.clone.1 | convolution fusion | flops 273154048 | bytes 6426629 | tf_op jit(solution)/shard_map/while/body/eval_jaxpr/bhqk,bqhd->bkhd/dot_general | solution.py:105
  292.1 2.2 multiply_reduce_fusion.11
  303.5 17.0 %collective-permute-done.3 = bf16[3,1,32,32,1,128]{5,3,2,4,1,0:T(8,128)(2,1)S(1)} collective-permute-done((bf16[3,1,32,32,1,128]{5,3,2,4,1,0:T(8,128)(2,1)S(1)}, bf16[3,1,32,32,1,128]{5,3,2,4,1,0:T(8,128)(2,1)S(1)}, u32[]{:S(2)}, u32[]{:S(2)}) %collective-permute-start.3) | collective-permute-done | bytes 786464 | tf_op jit(solution)/shard_map/ppermute | solution.py:17
  321.7 6.3 %all_to_all.148 = bf16[8,2,3,2,128,1,128]{6,4,0,2,3,5,1:T(8,128)(2,1)S(1)} all-to-all(bf16[8,2,3,2,128,1,128]{6,4,0,2,3,5,1:T(8,128)(2,1)S(1)} %copy.128), channel_id=1, replica_groups=mesh['win'=16,'seq_0'=4,'seq_1'=2,'seq_2'=2] {'seq_2'}, dimensions={1} | all-to-all | bytes 6291456 | tf_op jit(solution)/shard_map/all_to_all | solution.py:35
  328.4 51.5 %all_to_all.149 = bf16[8,2,3,2,128,1,128]{6,4,1,2,3,5,0:T(8,128)(2,1)S(1)} all-to-all(bf16[8,2,3,2,128,1,128]{6,4,1,2,3,5,0:T(8,128)(2,1)S(1)} %copy.129), channel_id=1, replica_groups=mesh['win'=16,'seq_0'=4,'seq_1'=2,'seq_2'=2] {'seq_0','seq_1'}, dimensions={0} | all-to-all | bytes 6291456 | tf_op jit(solution)/shard_map/all_to_all | solution.py:35
  (161 shorter events, 114.2 us)
Async XLA Ops:
  0.6 8.8 %copy-start.9 = (bf16[2,1,128,2048]{3,2,1,0:T(8,128)(2,1)S(1)}, bf16[2,1,128,2048]{3,2,1,0:T(8,128)(2,1)}, u32[]{:S(2)}) copy-start(bf16[2,1,128,2048]{3,2,1,0:T(8,128)(2,1)} %param.10) | copy-start | bytes 3145732
  3.3 18.5 %all-to-all-start.2 = ((bf16[1,128,16,128]{3,1,0,2:T(8,128)(2,1)}), bf16[1,128,16,128]{3,1,0,2:T(8,128)(2,1)S(1)}, u32[]{:S(2)}, u32[]{:S(2)}) async-start(bf16[1,128,16,128]{3,1,0,2:T(8,128)(2,1)} %copy.107), calls=%async_computation.2 | async-start | bytes 1048576 | tf_op jit(solution)/shard_map/all_to_all | solution.py:58
  21.8 15.9 %all-to-all-start.3 = ((bf16[1,128,16,128]{1,3,0,2:T(8,128)(2,1)}), bf16[1,128,16,128]{1,3,0,2:T(8,128)(2,1)S(1)}, u32[]{:S(2)}, u32[]{:S(2)}) async-start(bf16[1,128,16,128]{1,3,0,2:T(8,128)(2,1)} %bitcast.18), calls=%async_computation.3 | async-start | bytes 1048576 | tf_op jit(solution)/shard_map/all_to_all | solution.py:58
  37.7 15.9 %all-to-all-start = ((bf16[1,128,16,128]{1,3,0,2:T(8,128)(2,1)}), bf16[1,128,16,128]{1,3,0,2:T(8,128)(2,1)S(1)}, u32[]{:S(2)}, u32[]{:S(2)}) async-start(bf16[1,128,16,128]{1,3,0,2:T(8,128)(2,1)} %bitcast.1), calls=%async_computation | async-start | bytes 1048576 | tf_op jit(solution)/shard_map/all_to_all | solution.py:58
  53.7 15.9 %all-to-all-start.1 = ((bf16[1,128,16,128]{1,3,0,2:T(8,128)(2,1)}), bf16[1,128,16,128]{1,3,0,2:T(8,128)(2,1)S(1)}, u32[]{:S(2)}, u32[]{:S(2)}) async-start(bf16[1,128,16,128]{1,3,0,2:T(8,128)(2,1)} %bitcast.6), calls=%async_computation.1 | async-start | bytes 1048576 | tf_op jit(solution)/shard_map/all_to_all | solution.py:58
  69.6 53.5 %copy-start.6 = (bf16[1,128,16,128]{1,3,0,2:T(8,128)(2,1)}, bf16[1,128,16,128]{1,3,0,2:T(8,128)(2,1)S(1)}, u32[]{:S(2)}) copy-start(bf16[1,128,16,128]{1,3,0,2:T(8,128)(2,1)S(1)} %all-to-all-done.1) | copy-start | bytes 1572868
  69.6 15.9 %all-to-all-start.6 = ((bf16[1,128,16,128]{3,1,0,2:T(8,128)(2,1)}), bf16[1,128,16,128]{3,1,0,2:T(8,128)(2,1)S(1)}, u32[]{:S(2)}, u32[]{:S(2)}) async-start(bf16[1,128,16,128]{3,1,0,2:T(8,128)(2,1)} %copy.120), calls=%async_computation.6 | async-start | bytes 1048576 | tf_op jit(solution)/shard_map/all_to_all | solution.py:58
  85.5 39.0 %copy-start.7 = (bf16[1,128,16,128]{3,1,0,2:T(8,128)(2,1)}, bf16[1,128,16,128]{3,1,0,2:T(8,128)(2,1)S(1)}, u32[]{:S(2)}) copy-start(bf16[1,128,16,128]{3,1,0,2:T(8,128)(2,1)S(1)} %all-to-all-done.6) | copy-start | bytes 1572868
  85.5 15.9 %all-to-all-start.4 = ((bf16[1,128,16,128]{1,3,0,2:T(8,128)(2,1)}), bf16[1,128,16,128]{1,3,0,2:T(8,128)(2,1)S(1)}, u32[]{:S(2)}, u32[]{:S(2)}) async-start(bf16[1,128,16,128]{1,3,0,2:T(8,128)(2,1)} %bitcast.247), calls=%async_computation.4 | async-start | bytes 1048576 | tf_op jit(solution)/shard_map/all_to_all | solution.py:58
  101.4 23.1 %copy-start.8 = (bf16[1,128,16,128]{1,3,0,2:T(8,128)(2,1)}, bf16[1,128,16,128]{1,3,0,2:T(8,128)(2,1)S(1)}, u32[]{:S(2)}) copy-start(bf16[1,128,16,128]{1,3,0,2:T(8,128)(2,1)S(1)} %all-to-all-done.4) | copy-start | bytes 1572868
  101.4 16.6 %all-to-all-start.5 = ((bf16[1,128,16,128]{1,3,0,2:T(8,128)(2,1)}), bf16[1,128,16,128]{1,3,0,2:T(8,128)(2,1)}, u32[]{:S(2)}, u32[]{:S(2)}) async-start(bf16[1,128,16,128]{1,3,0,2:T(8,128)(2,1)} %bitcast.248), calls=%async_computation.5 | async-start | bytes 1048576 | tf_op jit(solution)/shard_map/all_to_all | solution.py:58
  118.0 16.6 %all-to-all-start.7 = ((bf16[1,128,16,128]{1,3,0,2:T(8,128)(2,1)}), bf16[1,128,16,128]{1,3,0,2:T(8,128)(2,1)}, u32[]{:S(2)}, u32[]{:S(2)}) async-start(bf16[1,128,16,128]{1,3,0,2:T(8,128)(2,1)} %bitcast.246), calls=%async_computation.7 | async-start | bytes 1048576 | tf_op jit(solution)/shard_map/all_to_all | solution.py:58
  123.1 15.1 %collective-permute-start = (bf16[1,32,32,1,128]{4,2,1,3,0:T(8,128)(2,1)}, bf16[1,32,32,1,128]{4,2,1,3,0:T(8,128)(2,1)}, u32[]{:S(2)}, u32[]{:S(2)}) collective-permute-start(bf16[1,32,32,1,128]{4,2,1,3,0:T(8,128)(2,1)} %get-tuple-element.230), channel_id=1, source_target_pairs={{16,0},{32,16},{48,32},{64,48},{80,64},{96,80},{112,96},{128,112},... | collective-permute-start | bytes 786440 | tf_op jit(solution)/shard_map/ppermute | solution.py:17
  126.3 96.2 %collective-permute-start.2 = (bf16[1,32,32,1,128]{4,2,1,3,0:T(8,128)(2,1)}, bf16[1,32,32,1,128]{4,2,1,3,0:T(8,128)(2,1)}, u32[]{:S(2)}, u32[]{:S(2)}) collective-permute-start(bf16[1,32,32,1,128]{4,2,1,3,0:T(8,128)(2,1)} %get-tuple-element.232), channel_id=1, source_target_pairs={{16,0},{32,16},{48,32},{64,48},{80,64},{96,80},{112,96},{128,112},... | collective-permute-start | bytes 786440 | tf_op jit(solution)/shard_map/ppermute | solution.py:17
  145.8 2.0 copy-start
  148.6 4.6 %copy-start.1 = (f32[512,2048]{1,0:T(8,128)S(1)}, f32[512,2048]{1,0:T(8,128)}, u32[]{:S(2)}) copy-start(f32[512,2048]{1,0:T(8,128)} %copy-done) | copy-start | bytes 12582916 | tf_op jit(solution)/shard_map/while
  148.6 4.6 %copy-start.11 = (bf16[1,2048,1,128]{3,1,2,0:T(8,128)(2,1)S(1)}, bf16[1,2048,1,128]{3,1,2,0:T(8,128)(2,1)}, u32[]{:S(2)}) copy-start(bf16[1,2048,1,128]{3,1,2,0:T(8,128)(2,1)} %get-tuple-element.427) | copy-start | bytes 1572868 | tf_op jit(solution)/shard_map/while
  163.7 2.0 copy-start
  166.5 4.9 %copy-start.1 = (f32[512,2048]{1,0:T(8,128)S(1)}, f32[512,2048]{1,0:T(8,128)}, u32[]{:S(2)}) copy-start(f32[512,2048]{1,0:T(8,128)} %copy-done) | copy-start | bytes 12582916 | tf_op jit(solution)/shard_map/while
  166.6 4.9 %copy-start.11 = (bf16[1,2048,1,128]{3,1,2,0:T(8,128)(2,1)S(1)}, bf16[1,2048,1,128]{3,1,2,0:T(8,128)(2,1)}, u32[]{:S(2)}) copy-start(bf16[1,2048,1,128]{3,1,2,0:T(8,128)(2,1)} %get-tuple-element.427) | copy-start | bytes 1572868 | tf_op jit(solution)/shard_map/while
  182.0 2.0 copy-start
  184.8 4.9 %copy-start.1 = (f32[512,2048]{1,0:T(8,128)S(1)}, f32[512,2048]{1,0:T(8,128)}, u32[]{:S(2)}) copy-start(f32[512,2048]{1,0:T(8,128)} %copy-done) | copy-start | bytes 12582916 | tf_op jit(solution)/shard_map/while
  184.8 4.9 %copy-start.11 = (bf16[1,2048,1,128]{3,1,2,0:T(8,128)(2,1)S(1)}, bf16[1,2048,1,128]{3,1,2,0:T(8,128)(2,1)}, u32[]{:S(2)}) copy-start(bf16[1,2048,1,128]{3,1,2,0:T(8,128)(2,1)} %get-tuple-element.427) | copy-start | bytes 1572868 | tf_op jit(solution)/shard_map/while
  200.2 2.0 copy-start
  203.0 4.9 %copy-start.1 = (f32[512,2048]{1,0:T(8,128)S(1)}, f32[512,2048]{1,0:T(8,128)}, u32[]{:S(2)}) copy-start(f32[512,2048]{1,0:T(8,128)} %copy-done) | copy-start | bytes 12582916 | tf_op jit(solution)/shard_map/while
  203.0 4.9 %copy-start.11 = (bf16[1,2048,1,128]{3,1,2,0:T(8,128)(2,1)S(1)}, bf16[1,2048,1,128]{3,1,2,0:T(8,128)(2,1)}, u32[]{:S(2)}) copy-start(bf16[1,2048,1,128]{3,1,2,0:T(8,128)(2,1)} %get-tuple-element.427) | copy-start | bytes 1572868 | tf_op jit(solution)/shard_map/while
  218.5 83.6 %collective-permute-start.1 = (bf16[3,1,32,32,1,128]{5,3,2,4,1,0:T(8,128)(2,1)}, bf16[3,1,32,32,1,128]{5,3,2,4,1,0:T(8,128)(2,1)}, u32[]{:S(2)}, u32[]{:S(2)}) collective-permute-start(bf16[3,1,32,32,1,128]{5,3,2,4,1,0:T(8,128)(2,1)} %fusion.53), channel_id=1, source_target_pairs={{240,0},{0,16},{16,32},{32,48},{48,64},{64,80},{80,96},{96,112},{1... | collective-permute-start | bytes 2359304 | tf_op jit(solution)/shard_map/ppermute | solution.py:17
  230.0 2.0 copy-start.2
  232.8 4.6 %copy-start.3 = (f32[512,2048]{1,0:T(8,128)S(1)}, f32[512,2048]{1,0:T(8,128)}, u32[]{:S(2)}) copy-start(f32[512,2048]{1,0:T(8,128)} %copy-done.2) | copy-start | bytes 12582916 | tf_op jit(solution)/shard_map/while
  232.9 4.6 %copy-start.10 = (bf16[1,2048,1,128]{3,1,2,0:T(8,128)(2,1)S(1)}, bf16[1,2048,1,128]{3,1,2,0:T(8,128)(2,1)}, u32[]{:S(2)}) copy-start(bf16[1,2048,1,128]{3,1,2,0:T(8,128)(2,1)} %get-tuple-element.391) | copy-start | bytes 1572868 | tf_op jit(solution)/shard_map/while
  248.0 2.0 copy-start.2
  250.8 4.9 %copy-start.3 = (f32[512,2048]{1,0:T(8,128)S(1)}, f32[512,2048]{1,0:T(8,128)}, u32[]{:S(2)}) copy-start(f32[512,2048]{1,0:T(8,128)} %copy-done.2) | copy-start | bytes 12582916 | tf_op jit(solution)/shard_map/while
  250.8 4.9 %copy-start.10 = (bf16[1,2048,1,128]{3,1,2,0:T(8,128)(2,1)S(1)}, bf16[1,2048,1,128]{3,1,2,0:T(8,128)(2,1)}, u32[]{:S(2)}) copy-start(bf16[1,2048,1,128]{3,1,2,0:T(8,128)(2,1)} %get-tuple-element.391) | copy-start | bytes 1572868 | tf_op jit(solution)/shard_map/while
  266.2 2.0 copy-start.2
  269.0 4.9 %copy-start.3 = (f32[512,2048]{1,0:T(8,128)S(1)}, f32[512,2048]{1,0:T(8,128)}, u32[]{:S(2)}) copy-start(f32[512,2048]{1,0:T(8,128)} %copy-done.2) | copy-start | bytes 12582916 | tf_op jit(solution)/shard_map/while
  269.0 4.9 %copy-start.10 = (bf16[1,2048,1,128]{3,1,2,0:T(8,128)(2,1)S(1)}, bf16[1,2048,1,128]{3,1,2,0:T(8,128)(2,1)}, u32[]{:S(2)}) copy-start(bf16[1,2048,1,128]{3,1,2,0:T(8,128)(2,1)} %get-tuple-element.391) | copy-start | bytes 1572868 | tf_op jit(solution)/shard_map/while
  284.4 2.0 copy-start.2
  287.3 4.9 %copy-start.3 = (f32[512,2048]{1,0:T(8,128)S(1)}, f32[512,2048]{1,0:T(8,128)}, u32[]{:S(2)}) copy-start(f32[512,2048]{1,0:T(8,128)} %copy-done.2) | copy-start | bytes 12582916 | tf_op jit(solution)/shard_map/while
  287.3 4.9 %copy-start.10 = (bf16[1,2048,1,128]{3,1,2,0:T(8,128)(2,1)S(1)}, bf16[1,2048,1,128]{3,1,2,0:T(8,128)(2,1)}, u32[]{:S(2)}) copy-start(bf16[1,2048,1,128]{3,1,2,0:T(8,128)(2,1)} %get-tuple-element.391) | copy-start | bytes 1572868 | tf_op jit(solution)/shard_map/while
  301.9 18.5 %collective-permute-start.3 = (bf16[3,1,32,32,1,128]{5,3,2,4,1,0:T(8,128)(2,1)S(1)}, bf16[3,1,32,32,1,128]{5,3,2,4,1,0:T(8,128)(2,1)S(1)}, u32[]{:S(2)}, u32[]{:S(2)}) collective-permute-start(bf16[3,1,32,32,1,128]{5,3,2,4,1,0:T(8,128)(2,1)S(1)} %fusion.52), channel_id=1, source_target_pairs={{240,0},{0,16},{16,32},{32,48},{48,64},{64,80},{80,96},{96,112},{1... | collective-permute-start | bytes 2359304 | tf_op jit(solution)/shard_map/ppermute | solution.py:17
  382.1 3.1 copy-start.5
  382.1 5.1 %copy-start.4 = (bf16[1,2,128,16,1,128]{5,2,1,0,3,4:T(8,128)(2,1)S(1)}, bf16[1,2,128,16,1,128]{5,2,1,0,3,4:T(8,128)(2,1)}, u32[]{:S(2)}) copy-start(bf16[1,2,128,16,1,128]{5,2,1,0,3,4:T(8,128)(2,1)} %get-tuple-element.214) | copy-start | bytes 3145732
where the time goes:
time: 392 us; the launch traced here: 389 us
  matrix products  92.3 us (24%)
  waiting for transfers between devices  90.6 us (23%)
  local copies, waits for them, and re-layouts  66.3 us (17%)
  blocking collectives  57.8 us (15%)
  starting transfers between devices  38.2 us (10%)
  other arithmetic  29.3 us (7%)
  loops' own time  13.8 us (4%)
    all_to_all x8, waiting for transfers between devices, items_in_groups(): lax.all_to_all(group, axis, split_axis=split_dim, concat_axis=concat_dim,...  72.1 us
    all_to_all x2, blocking collectives, exchange_in_order(): result = lax.all_to_all(result, axes[k], k, k, tiled=True)  57.8 us
    dot_general x8, matrix products, one_block(): jnp.einsum('bhqk,bqhd->bkhd', weights_low, grad_block, preferred_element_...  38.1 us
    all_to_all x8, starting transfers between devices, items_in_groups(): lax.all_to_all(group, axis, split_axis=split_dim, concat_axis=concat_dim,...  32.5 us
    ppermute x4, waiting for transfers between devices, passed_along(): return lax.ppermute(block, axis, route)  18.5 us
    dot_general x8, matrix products, one_block(): jnp.einsum('bqhd,bkhd->bhqk', grad_block, value_heads, preferred_element_...  17.7 us
    while x48, local copies, waits for them, and re-layouts  16 us
    another operation x2, loops' own time, window_grads(): lax.scan(one_block, (zero_acc, zero_acc), starts)  13.8 us
  transfers between devices with their start and end apart: 12, of which 10 were waited for; matrix products, arithmetic and copies ran while one was open for 41% of the time, Pallas kernels for 0%

commit v1 on v0

v1 whole, which is shorter than its diff:
```python
import jax
import jax.numpy as jnp
from jax import lax
from jax.experimental import pallas as pl
from jax.experimental.pallas import tpu as pltpu
from jax.sharding import PartitionSpec as P

F32, BF16 = jnp.float32, jnp.bfloat16
MESH = pl.DeviceIdType.MESH
SAMPLES, HEADS, HDIM, D = 2, 16, 128, 2048
WINS, SEQS = 16, 16
TOKENS = 2048
GROUPS, MEMBERS = 4, 4
ROWS_HERE, HALVES, HALF = 2, 2, 32
CHUNK = GROUPS * ROWS_HERE * HALVES * HALF
FACTOR = HDIM**-0.5
LOG2E = 1.4426950408889634


def dot(a, b, ca, cb):
    return lax.dot_general(a, b, (((ca,), (cb,)), ((), ())), preferred_element_type=F32)


def rows_of(block):
    return block.reshape(-1, HDIM)


def kernel(
    q, k, v, g, dq_out, dk_out, dv_out, got, made, key_total, value_total, key_t, weights, products,
    in_sem, in_send, out_sem, out_send,
):
    win = lax.axis_index("win")
    seq = lax.axis_index("seq")
    group, member = lax.div(seq, MEMBERS), lax.rem(seq, MEMBERS)
    west, east = lax.rem(win + WINS - 1, WINS), lax.rem(win + 1, WINS)

    barrier = pltpu.get_barrier_semaphore()

    def greet(n, carry):
        peer = lax.rem(seq + n, SEQS)
        for side in (west, east):
            pl.semaphore_signal(barrier, inc=1, device_id={"win": side, "seq": peer}, device_id_type=MESH)

        @pl.when(n > 0)
        def _():
            pl.semaphore_signal(barrier, inc=1, device_id={"win": win, "seq": peer}, device_id_type=MESH)

        return carry

    lax.fori_loop(0, SEQS, greet, 0)
    pl.semaphore_wait(barrier, 3 * SEQS - 1)

    def send(src, dst, send_sem, recv_sem, to_win, to_seq):
        pltpu.make_async_remote_copy(
            src_ref=src,
            dst_ref=dst,
            send_sem=send_sem,
            recv_sem=recv_sem,
            device_id={"win": to_win, "seq": to_seq},
            device_id_type=MESH,
        ).start()

    def peer_at(n):
        over = lax.rem(n + 1, 4)
        across = lax.rem(n + lax.div(n, 4), 2)
        core = 1 - lax.div(n, 8)
        to_group = lax.rem(group + over, GROUPS)
        to_high = lax.rem(lax.div(member, 2) + across, 2)
        to_core = lax.rem(lax.rem(member, 2) + core, 2)
        return to_group * MEMBERS + to_high * 2 + to_core

    moved_group = lax.rem(group + 2, GROUPS)

    def send_inputs(b):
        def step(n, carry):
            peer = peer_at(n)
            columns = pl.ds(pl.multiple_of(peer * HDIM, HDIM), HDIM)
            send(
                g.at[b, :, 0, :, columns],
                got.at[b, 3, moved_group, member, :, 1],
                in_send.at[b, 4],
                in_sem.at[b],
                west,
                peer,
            )

            @pl.when(n < SEQS - 1)
            def _():
                for a, array in enumerate((q, k, v)):
                    send(
                        array.at[b, :, :, :, columns],
                        got.at[b, a, group, member],
                        in_send.at[b, a],
                        in_sem.at[b],
                        win,
                        peer,
                    )
                send(
                    g.at[b, :, 1, :, columns],
                    got.at[b, 3, moved_group, member, :, 0],
                    in_send.at[b, 3],
                    in_sem.at[b],
                    win,
                    peer,
                )

            return carry

        lax.fori_loop(0, SEQS, step, 0)
        columns = pl.ds(pl.multiple_of(seq * HDIM, HDIM), HDIM)
        for a, array in enumerate((q, k, v)):
            pltpu.make_async_copy(array.at[b, :, :, :, columns], got.at[b, a, group, member], in_sem.at[b]).start()
        pltpu.make_async_copy(
            g.at[b, :, 1, :, columns], got.at[b, 3, moved_group, member, :, 0], in_sem.at[b]
        ).start()

    my_columns = pl.ds(pl.multiple_of(seq * HDIM, HDIM), HDIM)
    outs = (dq_out, dk_out, dv_out)

    def send_gradient(b, a, to_group, to_member):
        peer = to_group * MEMBERS + to_member
        at_group = lax.rem(to_group + 2, GROUPS)
        here = outs[a].at[b, :, 1, :, my_columns]
        send(
            made.at[b, a, at_group, to_member, :, 1],
            outs[a].at[b, :, 0, :, my_columns],
            out_send.at[b, a, 1],
            out_sem.at[a],
            east,
            peer,
        )

        @pl.when(peer != seq)
        def _():
            send(made.at[b, a, at_group, to_member, :, 0], here, out_send.at[b, a, 0], out_sem.at[a], win, peer)

        @pl.when(peer == seq)
        def _():
            pltpu.make_async_copy(made.at[b, a, at_group, to_member, :, 0], here, out_sem.at[a]).start()

    def grads(b):
        key_total[...] = jnp.zeros_like(key_total)
        value_total[...] = jnp.zeros_like(value_total)
        key_t[...] = rows_of(got[b, 1]).T

        def block(j, carry):
            query = rows_of(got[b, 0, :, j])
            grad = rows_of(got[b, 3, :, j])
            top = jnp.full((8, CHUNK), -jnp.inf, F32)
            for i in range(TOKENS // CHUNK):
                keys = pl.ds(i * CHUNK, CHUNK)
                scores = dot(rows_of(got[b, 1, i]), query, 1, 1)
                weights[keys] = scores
                top = jnp.maximum(top, jnp.max(scores.reshape(-1, 8, CHUNK), axis=0))
            top = jnp.max(top, axis=0, keepdims=True) * (FACTOR * LOG2E)
            total = jnp.zeros((8, CHUNK), F32)
            row_dot = jnp.zeros((8, CHUNK), F32)
            for i in range(TOKENS // CHUNK):
                keys = pl.ds(i * CHUNK, CHUNK)
                weight = jnp.exp2(weights[keys] * (FACTOR * LOG2E) - top)
                product = weight * dot(rows_of(got[b, 2, i]), grad, 1, 1)
                total = total + jnp.sum(weight.reshape(-1, 8, CHUNK), axis=0)
                row_dot = row_dot + jnp.sum(product.reshape(-1, 8, CHUNK), axis=0)
                weights[keys] = weight
                products[keys] = product
            share = 1.0 / jnp.sum(total, axis=0, keepdims=True)
            row_dot = jnp.sum(row_dot, axis=0, keepdims=True) * share * share
            query_grad = jnp.zeros((HDIM, CHUNK), F32)
            for i in range(TOKENS // CHUNK):
                keys = pl.ds(i * CHUNK, CHUNK)
                weight = weights[keys]
                low = (weight * share).astype(BF16)
                score_grad = (products[keys] * share - weight * row_dot).astype(BF16)
                value_total[keys] += dot(low, grad, 1, 0)
                key_total[keys] += dot(score_grad, query, 1, 0)
                query_grad = query_grad + dot(key_t[:, keys], score_grad, 1, 0)
            made[b, 0, :, j] = (query_grad * FACTOR).T.astype(BF16).reshape(GROUPS, ROWS_HERE, HALVES, HALF, HDIM)
            for n in range(GROUPS):
                send_gradient(b, 0, lax.rem(group + n + 1, GROUPS), j)
            return carry

        lax.fori_loop(0, MEMBERS, block, 0)
        whole = (GROUPS, MEMBERS, ROWS_HERE, HALVES, HALF, HDIM)
        made[b, 1] = (key_total[...] * FACTOR).astype(BF16).reshape(whole)
        made[b, 2] = value_total[...].astype(BF16).reshape(whole)

        def step(n, carry):
            peer = peer_at(n)
            for a in (1, 2):
                send_gradient(b, a, lax.div(peer, MEMBERS), lax.rem(peer, MEMBERS))
            return carry

        lax.fori_loop(0, SEQS, step, 0)

    for b in range(SAMPLES):
        send_inputs(b)

    def sample(b, carry):
        pltpu.make_async_copy(got.at[b], got.at[b], in_sem.at[b]).wait()
        grads(b)
        return carry

    lax.fori_loop(0, SAMPLES, sample, 0)

    def all_sent(ref, sem):
        pltpu.make_async_copy(ref, ref, sem).wait()

    others = pl.ds(0, SEQS - 1)
    for a in range(3):
        pltpu.make_async_copy(outs[a], outs[a], out_sem.at[a]).wait()
    for b in range(SAMPLES):
        for a in range(3):
            all_sent(q.at[b, :, :, :, pl.ds(0, (SEQS - 1) * HDIM)], in_send.at[b, a])
        all_sent(q.at[b, :, 0, :, pl.ds(0, (SEQS - 1) * HDIM)], in_send.at[b, 3])
        all_sent(q.at[b, :, 0], in_send.at[b, 4])
        for a in range(3):
            all_sent(q.at[b, :, 0, :, pl.ds(0, (SEQS - 1) * HDIM)], out_send.at[b, a, 0])
            all_sent(q.at[b, :, 0], out_send.at[b, a, 1])


def on_device(queries, key_states, value_states, out_grad):
    shape = (SAMPLES, ROWS_HERE, HALVES, HALF, D)
    arrays = [a.reshape(shape) for a in (queries, key_states, value_states, out_grad)]
    tokens = (GROUPS, MEMBERS, ROWS_HERE, HALVES, HALF, HDIM)
    results = pl.pallas_call(
        kernel,
        out_shape=[jax.ShapeDtypeStruct(shape, BF16)] * 3,
        in_specs=[pl.BlockSpec(memory_space=pltpu.HBM)] * 4,
        out_specs=[pl.BlockSpec(memory_space=pltpu.HBM)] * 3,
        scratch_shapes=[
            pltpu.VMEM((SAMPLES, 4, *tokens), BF16),
            pltpu.VMEM((SAMPLES, 3, *tokens), BF16),
            pltpu.VMEM((TOKENS, HDIM), F32),
            pltpu.VMEM((TOKENS, HDIM), F32),
            pltpu.VMEM((HDIM, TOKENS), BF16),
            pltpu.VMEM((TOKENS, CHUNK), F32),
            pltpu.VMEM((TOKENS, CHUNK), F32),
            pltpu.SemaphoreType.DMA((SAMPLES,)),
            pltpu.SemaphoreType.DMA((SAMPLES, 5)),
            pltpu.SemaphoreType.DMA((3,)),
            pltpu.SemaphoreType.DMA((SAMPLES, 3, 2)),
        ],
        compiler_params=pltpu.CompilerParams(collective_id=0, has_side_effects=True, vmem_limit_bytes=56 * 2**20),
        cost_estimate=pl.CostEstimate(flops=10 * 2 * TOKENS * TOKENS * HDIM, bytes_accessed=7 * 2**20, transcendentals=2 * TOKENS * TOKENS),
        name="window_backward",
    )(*arrays)
    return tuple(r.reshape(queries.shape) for r in results)


def solution(mesh):
    spec = P(None, "win", "seq", None)
    return jax.shard_map(on_device, mesh=mesh, in_specs=(spec,) * 4, out_specs=(spec,) * 3, check_vma=False)
```

time: 392 us -> 114 us (0.29)
  Pallas kernels: 0 us -> 106 us
  matrix products: 92.3 us -> 0 us
  waiting for transfers between devices: 90.6 us -> 0 us
  local copies, waits for them, and re-layouts: 66.3 us -> 4.97 us
  blocking collectives: 57.8 us -> 0 us
  starting transfers between devices: 38.2 us -> 0 us
  other arithmetic: 29.3 us -> 0 us
  loops' own time: 13.8 us -> 0 us
    pallas_call x0 -> x1, Pallas kernels: none -> 106 us  [on_device(): pl.pallas_call(kernel, out_shape=[jax.ShapeDtypeStruct(shape, BF16)] * 3,...]
    dot_general x40 -> x0, matrix products: 92.3 us -> none  [the longest x8 38.1 us: one_block(): jnp.einsum('bhqk,bqhd->bkhd', weights_low, grad_block, preferred_element_...]
    all_to_all x8 -> x0, waiting for transfers between devices: 72.1 us -> none  [items_in_groups(): lax.all_to_all(group, axis, split_axis=split_dim, concat_axis=concat_dim,...]
    all_to_all x2 -> x0, blocking collectives: 57.8 us -> none  [exchange_in_order(): result = lax.all_to_all(result, axes[k], k, k, tiled=True)]
    all_to_all x8 -> x0, starting transfers between devices: 32.5 us -> none  [items_in_groups(): lax.all_to_all(group, axis, split_axis=split_dim, concat_axis=concat_dim,...]
    while x52 -> x0, local copies, waits for them, and re-layouts: 19.6 us -> none
    ppermute x4 -> x0, waiting for transfers between devices: 18.5 us -> none  [passed_along(): return lax.ppermute(block, axis, route)]
    slice x14 -> x0, local copies, waits for them, and re-layouts: 16.3 us -> none  [the longest x6 8.56 us: items_in_groups(): lax.slice_in_dim(a, k * (items // count), (k + 1) * (items // count), axi...]
  transfers between devices with their start and end apart: 12 -> 0, of which waited for: 10 -> 0; matrix products, arithmetic and copies ran while one was open for 41% -> 0% of each run, Pallas kernels for 0% -> 0%
where the time goes in v1:
time: 114 us; the launch traced here: 112 us
  Pallas kernels  106 us (93%)
  local copies, waits for them, and re-layouts  4.97 us (4%)
    pallas_call x1, Pallas kernels, on_device(): pl.pallas_call(kernel, out_shape=[jax.ShapeDtypeStruct(shape, BF16)] * 3,...  106 us
    unnamed x7, local copies, waits for them, and re-layouts  4.97 us

profile of v1, /device:TPU:104, one launch (start us, length us, event | category | flops | bytes accessed | tf_op | source)
XLA Modules:
  0.0 111.7 jit_solution(11122969406987700848)
XLA Ops:
  0.6 106.1 %window_backward.1 = (bf16[2,2,2,32,2048]{4,3,2,1,0:T(8,128)(2,1)}, bf16[2,2,2,32,2048]{4,3,2,1,0:T(8,128)(2,1)}, bf16[2,2,2,32,2048]{4,3,2,1,0:T(8,128)(2,1)}) custom-call(bf16[2,2,2,32,2048]{4,3,2,1,0:T(8,128)(2,1)} %bitcast.16, bf16[2,2,2,32,2048]{4,3,2,1,0:T(8,128)(2,1)} %bitcast.17, bf16[2,2,2,32,2048]{4,3,2,1,0:T(8,128)(2,1)} %bitcast.18, ...), custom_call_target="tpu_custom_call" | custom-call | flops 10737418240 | bytes 7340032 | tf_op jit(solution)/shard_map/window_backward/pallas_call | solution.py:225
  106.7 0.0 copy-start.1
  106.7 2.4 %copy.13 = bf16[2,1,128,2048]{3,2,1,0:T(8,128)(2,1)} copy(bf16[2,1,128,2048]{3,2,1,0:T(8,128)(2,1)} %bitcast.15) | data formatting | bytes 2097152
  109.1 0.0 copy-done.1
  109.1 0.0 copy-start
  109.1 1.0 copy.14
  110.1 0.6 copy-done
  110.7 1.0 copy.15
Async XLA Ops:
  106.7 2.4 %copy-start.1 = (bf16[2,2,2,32,2048]{4,3,2,1,0:T(8,128)(2,1)S(1)}, bf16[2,2,2,32,2048]{4,3,2,1,0:T(8,128)(2,1)}, u32[]{:S(2)}) copy-start(bf16[2,2,2,32,2048]{4,3,2,1,0:T(8,128)(2,1)} %get-tuple-element.7) | copy-start | bytes 3145732
  109.1 1.6 %copy-start = (bf16[2,2,2,32,2048]{4,3,2,1,0:T(8,128)(2,1)S(1)}, bf16[2,2,2,32,2048]{4,3,2,1,0:T(8,128)(2,1)}, u32[]{:S(2)}) copy-start(bf16[2,2,2,32,2048]{4,3,2,1,0:T(8,128)(2,1)} %get-tuple-element.8) | copy-start | bytes 3145732

commit v2 on v1

--- a/solution.py
+++ b/solution.py
@@ -32,23 +32,46 @@
     win = lax.axis_index("win")
     seq = lax.axis_index("seq")
     group, member = lax.div(seq, MEMBERS), lax.rem(seq, MEMBERS)
-    west, east = lax.rem(win + WINS - 1, WINS), lax.rem(win + 1, WINS)
+    core = lax.rem(member, 2)
+
+    def place_of(window, head_core):
+        return window + head_core * (1 - 2 * lax.rem(window, 2))
+
+    work = place_of(win, core)
+    work_east = lax.rem(work + 1, WINS)
+    west = lax.rem(win + WINS - 1, WINS)
+    stays = core == 0
+    stays_west = (core == 1) & (lax.rem(win, 2) == 1)
 
     barrier = pltpu.get_barrier_semaphore()
 
     def greet(n, carry):
         peer = lax.rem(seq + n, SEQS)
-        for side in (west, east):
-            pl.semaphore_signal(barrier, inc=1, device_id={"win": side, "seq": peer}, device_id_type=MESH)
-
-        @pl.when(n > 0)
-        def _():
-            pl.semaphore_signal(barrier, inc=1, device_id={"win": win, "seq": peer}, device_id_type=MESH)
+        peer_core = lax.rem(peer, 2)
+        far = (n > 0) | jnp.logical_not(stays)
+        far_west = (n > 0) | jnp.logical_not(stays_west)
+
+        @pl.when(far)
+        def _():
+            for place in (place_of(win, peer_core), work):
+                pl.semaphore_signal(barrier, inc=1, device_id={"win": place, "seq": peer}, device_id_type=MESH)
+
+        @pl.when(far_west)
+        def _():
+            for place in (place_of(west, peer_core), work_east):
+                pl.semaphore_signal(barrier, inc=1, device_id={"win": place, "seq": peer}, device_id_type=MESH)
 
         return carry
 
     lax.fori_loop(0, SEQS, greet, 0)
-    pl.semaphore_wait(barrier, 3 * SEQS - 1)
+
+    @pl.when(stays | stays_west)
+    def _():
+        pl.semaphore_wait(barrier, 4 * SEQS - 2)
+
+    @pl.when(jnp.logical_not(stays | stays_west))
+    def _():
+        pl.semaphore_wait(barrier, 4 * SEQS)
 
     def send(src, dst, send_sem, recv_sem, to_win, to_seq):
         pltpu.make_async_remote_copy(
@@ -71,28 +94,33 @@
 
     moved_group = lax.rem(group + 2, GROUPS)
 
-    def send_inputs(b):
+    def send_inputs(b, first, last):
         def step(n, carry):
             peer = peer_at(n)
+            peer_core = lax.rem(peer, 2)
             columns = pl.ds(pl.multiple_of(peer * HDIM, HDIM), HDIM)
-            send(
-                g.at[b, :, 0, :, columns],
-                got.at[b, 3, moved_group, member, :, 1],
-                in_send.at[b, 4],
-                in_sem.at[b],
-                west,
-                peer,
-            )
-
-            @pl.when(n < SEQS - 1)
-            def _():
+
+            @pl.when((n < SEQS - 1) | jnp.logical_not(stays_west))
+            def _():
+                send(
+                    g.at[b, :, 0, :, columns],
+                    got.at[b, 3, moved_group, member, :, 1],
+                    in_send.at[b, 4],
+                    in_sem.at[b],
+                    place_of(west, peer_core),
+                    peer,
+                )
+
+            @pl.when((n < SEQS - 1) | jnp.logical_not(stays))
+            def _():
+                place = place_of(win, peer_core)
                 for a, array in enumerate((q, k, v)):
                     send(
                         array.at[b, :, :, :, columns],
                         got.at[b, a, group, member],
                         in_send.at[b, a],
                         in_sem.at[b],
-                        win,
+                        place,
                         peer,
                     )
                 send(
@@ -100,19 +128,32 @@
                     got.at[b, 3, moved_group, member, :, 0],
                     in_send.at[b, 3],
                     in_sem.at[b],
-                    win,
+                    place,
                     peer,
                 )
 
             return carry
 
-        lax.fori_loop(0, SEQS, step, 0)
+        lax.fori_loop(first, last, step, 0)
+
+    def own_inputs(b):
         columns = pl.ds(pl.multiple_of(seq * HDIM, HDIM), HDIM)
-        for a, array in enumerate((q, k, v)):
-            pltpu.make_async_copy(array.at[b, :, :, :, columns], got.at[b, a, group, member], in_sem.at[b]).start()
-        pltpu.make_async_copy(
-            g.at[b, :, 1, :, columns], got.at[b, 3, moved_group, member, :, 0], in_sem.at[b]
-        ).start()
+
+        @pl.when(stays)
+        def _():
+            for a, array in enumerate((q, k, v)):
+                pltpu.make_async_copy(
+                    array.at[b, :, :, :, columns], got.at[b, a, group, member], in_sem.at[b]
+                ).start()
+            pltpu.make_async_copy(
+                g.at[b, :, 1, :, columns], got.at[b, 3, moved_group, member, :, 0], in_sem.at[b]
+            ).start()
+
+        @pl.when(stays_west)
+        def _():
+            pltpu.make_async_copy(
+                g.at[b, :, 0, :, columns], got.at[b, 3, moved_group, member, :, 1], in_sem.at[b]
+            ).start()
 
     my_columns = pl.ds(pl.multiple_of(seq * HDIM, HDIM), HDIM)
     outs = (dq_out, dk_out, dv_out)
@@ -120,23 +161,20 @@
     def send_gradient(b, a, to_group, to_member):
         peer = to_group * MEMBERS + to_member
         at_group = lax.rem(to_group + 2, GROUPS)
-        here = outs[a].at[b, :, 1, :, my_columns]
-        send(
-            made.at[b, a, at_group, to_member, :, 1],
-            outs[a].at[b, :, 0, :, my_columns],
-            out_send.at[b, a, 1],
-            out_sem.at[a],
-            east,
-            peer,
+        parts = (
+            (1, outs[a].at[b, :, 0, :, my_columns], work_east, (peer == seq) & stays_west),
+            (0, outs[a].at[b, :, 1, :, my_columns], work, (peer == seq) & stays),
         )
-
-        @pl.when(peer != seq)
-        def _():
-            send(made.at[b, a, at_group, to_member, :, 0], here, out_send.at[b, a, 0], out_sem.at[a], win, peer)
-
-        @pl.when(peer == seq)
-        def _():
-            pltpu.make_async_copy(made.at[b, a, at_group, to_member, :, 0], here, out_sem.at[a]).start()
+        for half, place, to_win, at_home in parts:
+            part = made.at[b, a, at_group, to_member, :, half]
+
+            @pl.when(jnp.logical_not(at_home))
+            def _():
+                send(part, place, out_send.at[b, a, half], out_sem.at[a], to_win, peer)
+
+            @pl.when(at_home)
+            def _():
+                pltpu.make_async_copy(part, place, out_sem.at[a]).start()
 
     def grads(b):
         key_total[...] = jnp.zeros_like(key_total)
@@ -144,6 +182,10 @@
         key_t[...] = rows_of(got[b, 1]).T
 
         def block(j, carry):
+            @pl.when((b == 0) & (j == 0))
+            def _():
+                send_inputs(1, SEQS // 2, SEQS)
+
             query = rows_of(got[b, 0, :, j])
             grad = rows_of(got[b, 3, :, j])
             top = jnp.full((8, CHUNK), -jnp.inf, F32)
@@ -192,8 +234,10 @@
 
         lax.fori_loop(0, SEQS, step, 0)
 
+    send_inputs(0, 0, SEQS)
     for b in range(SAMPLES):
-        send_inputs(b)
+        own_inputs(b)
+    send_inputs(1, 0, SEQS // 2)
 
     def sample(b, carry):
         pltpu.make_async_copy(got.at[b], got.at[b], in_sem.at[b]).wait()
@@ -202,20 +246,28 @@
 
     lax.fori_loop(0, SAMPLES, sample, 0)
 
-    def all_sent(ref, sem):
-        pltpu.make_async_copy(ref, ref, sem).wait()
-
-    others = pl.ds(0, SEQS - 1)
     for a in range(3):
         pltpu.make_async_copy(outs[a], outs[a], out_sem.at[a]).wait()
+
+    def all_sent(whole, sem, one_stays):
+        most = whole.at[..., pl.ds(0, (SEQS - 1) * HDIM)]
+
+        @pl.when(one_stays)
+        def _():
+            pltpu.make_async_copy(most, most, sem).wait()
+
+        @pl.when(jnp.logical_not(one_stays))
+        def _():
+            pltpu.make_async_copy(whole, whole, sem).wait()
+
     for b in range(SAMPLES):
         for a in range(3):
-            all_sent(q.at[b, :, :, :, pl.ds(0, (SEQS - 1) * HDIM)], in_send.at[b, a])
-        all_sent(q.at[b, :, 0, :, pl.ds(0, (SEQS - 1) * HDIM)], in_send.at[b, 3])
-        all_sent(q.at[b, :, 0], in_send.at[b, 4])
+            all_sent(q.at[b], in_send.at[b, a], stays)
+        all_sent(q.at[b, :, 0], in_send.at[b, 3], stays)
+        all_sent(q.at[b, :, 0], in_send.at[b, 4], stays_west)
         for a in range(3):
-            all_sent(q.at[b, :, 0, :, pl.ds(0, (SEQS - 1) * HDIM)], out_send.at[b, a, 0])
-            all_sent(q.at[b, :, 0], out_send.at[b, a, 1])
+            all_sent(q.at[b, :, 0], out_send.at[b, a, 0], stays)
+            all_sent(q.at[b, :, 0], out_send.at[b, a, 1], stays_west)
 
 
 def on_device(queries, key_states, value_states, out_grad):
@@ -224,9 +276,9 @@
     tokens = (GROUPS, MEMBERS, ROWS_HERE, HALVES, HALF, HDIM)
     results = pl.pallas_call(
         kernel,
-        out_shape=[jax.ShapeDtypeStruct(shape, BF16)] * 3,
+        out_shape=[pltpu.VMEM(shape, BF16)] * 3,
         in_specs=[pl.BlockSpec(memory_space=pltpu.HBM)] * 4,
-        out_specs=[pl.BlockSpec(memory_space=pltpu.HBM)] * 3,
+        out_specs=[pl.BlockSpec(memory_space=pltpu.VMEM)] * 3,
         scratch_shapes=[
             pltpu.VMEM((SAMPLES, 4, *tokens), BF16),
             pltpu.VMEM((SAMPLES, 3, *tokens), BF16),
@@ -240,7 +292,7 @@
             pltpu.SemaphoreType.DMA((3,)),
             pltpu.SemaphoreType.DMA((SAMPLES, 3, 2)),
         ],
-        compiler_params=pltpu.CompilerParams(collective_id=0, has_side_effects=True, vmem_limit_bytes=56 * 2**20),
+        compiler_params=pltpu.CompilerParams(collective_id=0, has_side_effects=True, vmem_limit_bytes=58 * 2**20),
         cost_estimate=pl.CostEstimate(flops=10 * 2 * TOKENS * TOKENS * HDIM, bytes_accessed=7 * 2**20, transcendentals=2 * TOKENS * TOKENS),
         name="window_backward",
     )(*arrays)

time: 114 us -> 108 us (0.947)
  Pallas kernels: 106 us -> 103 us
  local copies, waits for them, and re-layouts: 4.97 us -> 2.91 us
    pallas_call x1, Pallas kernels: 106 us -> 103 us  [on_device(): pl.pallas_call(kernel, out_shape=[pltpu.VMEM(shape, BF16)] * 3, in_specs=...]
    unnamed x7 -> x3, local copies, waits for them, and re-layouts: 4.97 us -> 2.91 us
where the time goes in v2:
time: 108 us; the launch traced here: 106 us
  Pallas kernels  103 us (95%)
  local copies, waits for them, and re-layouts  2.91 us (3%)
    pallas_call x1, Pallas kernels, on_device(): pl.pallas_call(kernel, out_shape=[pltpu.VMEM(shape, BF16)] * 3, in_specs=...  103 us
    unnamed x3, local copies, waits for them, and re-layouts  2.91 us

profile of v2, /device:TPU:104, one launch (start us, length us, event | category | flops | bytes accessed | tf_op | source)
XLA Modules:
  0.0 106.4 jit_solution(14039429354241494605)
XLA Ops:
  0.6 102.8 %window_backward.1 = (bf16[2,2,2,32,2048]{4,3,2,1,0:T(8,128)(2,1)S(1)}, bf16[2,2,2,32,2048]{4,3,2,1,0:T(8,128)(2,1)S(1)}, bf16[2,2,2,32,2048]{4,3,2,1,0:T(8,128)(2,1)S(1)}) custom-call(bf16[2,2,2,32,2048]{4,3,2,1,0:T(8,128)(2,1)} %bitcast.16, bf16[2,2,2,32,2048]{4,3,2,1,0:T(8,128)(2,1)} %bitcast.17, bf16[2,2,2,32,2048]{4,3,2,1,0:T(8,128)(2,1)} %bitcast.18, ...), custom_call_target="tpu_custom_call" | custom-call | flops 10737418240 | bytes 7340032 | tf_op jit(solution)/shard_map/window_backward/pallas_call | solution.py:277
  103.5 1.0 copy.13
  104.4 1.0 copy.14
  105.4 1.0 copy.15

commit v3 on v2

--- a/solution.py
+++ b/solution.py
@@ -176,6 +176,19 @@
             def _():
                 pltpu.make_async_copy(part, place, out_sem.at[a]).start()
 
+    def send_totals(b, first, last):
+        def step(n, carry):
+            peer = peer_at(n)
+            for a in (1, 2):
+                send_gradient(b, a, lax.div(peer, MEMBERS), lax.rem(peer, MEMBERS))
+            return carry
+
+        lax.fori_loop(first, last, step, 0)
+
+    def send_rows(b, to_member):
+        for n in range(GROUPS):
+            send_gradient(b, 0, lax.rem(group + n + 1, GROUPS), to_member)
+
     def grads(b):
         key_total[...] = jnp.zeros_like(key_total)
         value_total[...] = jnp.zeros_like(value_total)
@@ -185,6 +198,10 @@
             @pl.when((b == 0) & (j == 0))
             def _():
                 send_inputs(1, SEQS // 2, SEQS)
+
+            @pl.when(b == 1)
+            def _():
+                send_totals(0, j * 4, (j + 1) * 4)
 
             query = rows_of(got[b, 0, :, j])
             grad = rows_of(got[b, 3, :, j])
@@ -205,6 +222,11 @@
                 row_dot = row_dot + jnp.sum(product.reshape(-1, 8, CHUNK), axis=0)
                 weights[keys] = weight
                 products[keys] = product
+
+            @pl.when(j > 0)
+            def _():
+                send_rows(b, j - 1)
+
             share = 1.0 / jnp.sum(total, axis=0, keepdims=True)
             row_dot = jnp.sum(row_dot, axis=0, keepdims=True) * share * share
             query_grad = jnp.zeros((HDIM, CHUNK), F32)
@@ -217,8 +239,10 @@
                 key_total[keys] += dot(score_grad, query, 1, 0)
                 query_grad = query_grad + dot(key_t[:, keys], score_grad, 1, 0)
             made[b, 0, :, j] = (query_grad * FACTOR).T.astype(BF16).reshape(GROUPS, ROWS_HERE, HALVES, HALF, HDIM)
-            for n in range(GROUPS):
-                send_gradient(b, 0, lax.rem(group + n + 1, GROUPS), j)
+            @pl.when(j == MEMBERS - 1)
+            def _():
+                send_rows(b, j)
+
             return carry
 
         lax.fori_loop(0, MEMBERS, block, 0)
@@ -226,13 +250,9 @@
         made[b, 1] = (key_total[...] * FACTOR).astype(BF16).reshape(whole)
         made[b, 2] = value_total[...].astype(BF16).reshape(whole)
 
-        def step(n, carry):
-            peer = peer_at(n)
-            for a in (1, 2):
-                send_gradient(b, a, lax.div(peer, MEMBERS), lax.rem(peer, MEMBERS))
-            return carry
-
-        lax.fori_loop(0, SEQS, step, 0)
+        @pl.when(b == 1)
+        def _():
+            send_totals(1, 0, SEQS)
 
     send_inputs(0, 0, SEQS)
     for b in range(SAMPLES):

time: 108 us -> 102 us (0.944)
  Pallas kernels: 103 us -> 96.5 us
    pallas_call x1, Pallas kernels: 103 us -> 96.5 us  [on_device(): pl.pallas_call(kernel, out_shape=[pltpu.VMEM(shape, BF16)] * 3, in_specs=...]
where the time goes in v3:
time: 102 us; the launch traced here: 100 us
  Pallas kernels  96.5 us (95%)
  local copies, waits for them, and re-layouts  2.91 us (3%)
    pallas_call x1, Pallas kernels, on_device(): pl.pallas_call(kernel, out_shape=[pltpu.VMEM(shape, BF16)] * 3, in_specs=...  96.5 us
    unnamed x3, local copies, waits for them, and re-layouts  2.91 us

profile of v3, /device:TPU:104, one launch (start us, length us, event | category | flops | bytes accessed | tf_op | source)
XLA Modules:
  0.0 100.0 jit_solution(13627335561108024406)
XLA Ops:
  0.6 96.5 %window_backward.1 = (bf16[2,2,2,32,2048]{4,3,2,1,0:T(8,128)(2,1)S(1)}, bf16[2,2,2,32,2048]{4,3,2,1,0:T(8,128)(2,1)S(1)}, bf16[2,2,2,32,2048]{4,3,2,1,0:T(8,128)(2,1)S(1)}) custom-call(bf16[2,2,2,32,2048]{4,3,2,1,0:T(8,128)(2,1)} %bitcast.16, bf16[2,2,2,32,2048]{4,3,2,1,0:T(8,128)(2,1)} %bitcast.17, bf16[2,2,2,32,2048]{4,3,2,1,0:T(8,128)(2,1)} %bitcast.18, ...), custom_call_target="tpu_custom_call" | custom-call | flops 10737418240 | bytes 7340032 | tf_op jit(solution)/shard_map/window_backward/pallas_call | solution.py:297
  97.1 1.0 copy.13
  98.1 1.0 copy.14
  99.0 1.0 copy.15

commit v4 on v3

--- a/solution.py
+++ b/solution.py
@@ -288,6 +288,19 @@
         for a in range(3):
             all_sent(q.at[b, :, 0], out_send.at[b, a, 0], stays)
             all_sent(q.at[b, :, 0], out_send.at[b, a, 1], stays_west)
+
+
+def settle(*refs):
+    ins, outs, sem = refs[:3], refs[3:6], refs[6]
+    copies = [
+        pltpu.make_async_copy(a.at[b], o.at[b], sem.at[i, b])
+        for i, (a, o) in enumerate(zip(ins, outs))
+        for b in range(SAMPLES)
+    ]
+    for copy in copies:
+        copy.start()
+    for copy in copies:
+        copy.wait()
 
 
 def on_device(queries, key_states, value_states, out_grad):
@@ -316,6 +329,15 @@
         cost_estimate=pl.CostEstimate(flops=10 * 2 * TOKENS * TOKENS * HDIM, bytes_accessed=7 * 2**20, transcendentals=2 * TOKENS * TOKENS),
         name="window_backward",
     )(*arrays)
+    results = pl.pallas_call(
+        settle,
+        out_shape=[jax.ShapeDtypeStruct(shape, BF16)] * 3,
+        in_specs=[pl.BlockSpec(memory_space=pltpu.VMEM)] * 3,
+        out_specs=[pl.BlockSpec(memory_space=pltpu.HBM)] * 3,
+        scratch_shapes=[pltpu.SemaphoreType.DMA((3, SAMPLES))],
+        compiler_params=pltpu.CompilerParams(vmem_limit_bytes=8 * 2**20),
+        name="settle",
+    )(*results)
     return tuple(r.reshape(queries.shape) for r in results)
 
 

time: 102 us -> 100 us (0.980)
  local copies, waits for them, and re-layouts: 2.91 us -> 0 us
  Pallas kernels: 96.5 us -> 98.2 us
    unnamed x3 -> x0, local copies, waits for them, and re-layouts: 2.91 us -> none
    pallas_call x0 -> x1, Pallas kernels: none -> 1.71 us  [on_device(): pl.pallas_call(settle, out_shape=[jax.ShapeDtypeStruct(shape, BF16)] * 3,...]
where the time goes in v4:
time: 100 us; the launch traced here: 98.8 us
  Pallas kernels  98.2 us (98%)
    pallas_call x1, Pallas kernels, on_device(): pl.pallas_call(kernel, out_shape=[pltpu.VMEM(shape, BF16)] * 3, in_specs=...  96.5 us

profile of v4, /device:TPU:104, one launch (start us, length us, event | category | flops | bytes accessed | tf_op | source)
XLA Modules:
  0.0 98.8 jit_solution(12076517820167645757)
XLA Ops:
  0.6 96.5 %window_backward.1 = (bf16[2,2,2,32,2048]{4,3,2,1,0:T(8,128)(2,1)S(1)}, bf16[2,2,2,32,2048]{4,3,2,1,0:T(8,128)(2,1)S(1)}, bf16[2,2,2,32,2048]{4,3,2,1,0:T(8,128)(2,1)S(1)}) custom-call(bf16[2,2,2,32,2048]{4,3,2,1,0:T(8,128)(2,1)} %bitcast.13, bf16[2,2,2,32,2048]{4,3,2,1,0:T(8,128)(2,1)} %bitcast.14, bf16[2,2,2,32,2048]{4,3,2,1,0:T(8,128)(2,1)} %bitcast.15, ...), custom_call_target="tpu_custom_call" | custom-call | flops 10737418240 | bytes 7340032 | tf_op jit(solution)/shard_map/window_backward/pallas_call | solution.py:310
  97.1 1.7 %settle.1 = (bf16[2,2,2,32,2048]{4,3,2,1,0:T(8,128)(2,1)}, bf16[2,2,2,32,2048]{4,3,2,1,0:T(8,128)(2,1)}, bf16[2,2,2,32,2048]{4,3,2,1,0:T(8,128)(2,1)}) custom-call(bf16[2,2,2,32,2048]{4,3,2,1,0:T(8,128)(2,1)S(1)} %get-tuple-element.9.refs_0_, bf16[2,2,2,32,2048]{4,3,2,1,0:T(8,128)(2,1)S(1)} %get-tuple-element.10.refs_1_, ...), custom_call_target="tpu_custom_call" | custom-call | tf_op jit(solution)/shard_map/settle/pallas_call | solution.py:332
